TPU v7x, 256 devices: a whole 4x4x8 slice. The times are simulated.
256 devices in a mesh: tm: 32 (over y, z_lo, core), head: 8 (over z_hi, x).
Axes of the slice: x: 4, y: 4, z: 8 (z_hi: 2, z_lo: 4; z = z_hi * 4 + z_lo), core: 2. Of those that a mesh axis runs over, the one named last changes fastest.
Arguments:
- latents: bfloat16 [16384, 3072], P(('tm', 'head')), may hold values from -6 to 6
- cotangent: bfloat16 [16384, 3072], P(('tm', 'head')), may hold values from -6 to 6
- norm_gain: float32 [3072], replicated, may hold values from 0.1 to 1.9
- w_qkv: bfloat16 [3072, 3, 3072], P(None, None, 'head'), may hold values from -0.114763592 to 0.114763592
- w_out: bfloat16 [3072, 3072], P('head'), may hold values from -0.109375 to 0.109375
Outputs:
- input_grad: bfloat16 [16384, 3072], P(('tm', 'head'))
All inputs are finite; a program needn't handle non-finite values.
Results may differ from a plain program's by a relative error of at most 0.012.
Values may be sent and summed in bfloat16 or wider, within the bound.
A program may use at most 128 MiB of HBM per device.

v0:
```python
import jax
import jax.numpy as jnp
from jax import lax
from jax.sharding import PartitionSpec as P

HEAD_DIM = 128
EPSILON = 1e-06


def from_behind(block, axis, distance):
    devices = range(lax.axis_size(axis))
    route = [(i - distance, i) for i in devices if i - distance in devices]
    return lax.ppermute(block, axis, route)


def scores_of(queries, keys):
    return jnp.einsum(
        "phe,khe->hpk", queries, keys, preferred_element_type=jnp.float32
    ) * HEAD_DIM ** (-0.5)


def shards(latents, cotangent, norm_gain, w_qkv, w_out):
    feature_count = latents.shape[1]
    local_width = w_qkv.shape[2]
    heads_here = local_width // HEAD_DIM
    scale = HEAD_DIM ** (-0.5)
    latent_f = latents.astype(jnp.float32)
    inv_rms = lax.rsqrt(jnp.mean(latent_f * latent_f, axis=-1, keepdims=True) + EPSILON)
    normed = latent_f * inv_rms
    hidden = (normed * norm_gain).astype(jnp.bfloat16)
    flat_w = w_qkv.reshape(feature_count, 3 * local_width)
    projected = jnp.dot(
        lax.all_gather(hidden, "head", axis=0, tiled=True),
        flat_w,
        preferred_element_type=jnp.float32,
    ).astype(jnp.bfloat16)
    frame_len = projected.shape[0]
    shape3 = (frame_len, heads_here, HEAD_DIM)
    queries = projected[:, :local_width].reshape(shape3)
    keys_own = projected[:, local_width : 2 * local_width].reshape(shape3)
    values_own = projected[:, 2 * local_width :].reshape(shape3)
    keys_prev, values_prev = from_behind((keys_own, values_own), "tm", 1)
    has_prev = (lax.axis_index("tm") > 0).astype(jnp.float32)
    grad_attn = (
        lax.dot_general(
            lax.all_gather(cotangent, "head", axis=0, tiled=True),
            w_out,
            (((1,), (1,)), ((), ())),
            preferred_element_type=jnp.float32,
        )
        .astype(jnp.bfloat16)
        .reshape(shape3)
    )
    own_s = scores_of(queries, keys_own)
    prev_s = scores_of(queries, keys_prev)
    row_top = jnp.maximum(
        jnp.max(own_s, axis=-1), jnp.where(has_prev > 0.5, jnp.max(prev_s, axis=-1), -1e30)
    )
    own_e = jnp.exp(own_s - row_top[..., None])
    prev_e = jnp.exp(prev_s - row_top[..., None]) * has_prev
    row_total = jnp.sum(own_e, axis=-1) + jnp.sum(prev_e, axis=-1)
    own_p = own_e / row_total[..., None]
    prev_p = prev_e / row_total[..., None]
    own_dp = jnp.einsum("phe,khe->hpk", grad_attn, values_own, preferred_element_type=jnp.float32)
    prev_dp = jnp.einsum("phe,khe->hpk", grad_attn, values_prev, preferred_element_type=jnp.float32)
    row_delta = jnp.sum(own_p * own_dp, axis=-1) + jnp.sum(prev_p * prev_dp, axis=-1)
    own_ds = (own_p * (own_dp - row_delta[..., None]) * scale).astype(jnp.bfloat16)
    prev_ds = (prev_p * (prev_dp - row_delta[..., None]) * scale).astype(jnp.bfloat16)
    grad_query = (
        jnp.einsum("hpk,khe->phe", own_ds, keys_own, preferred_element_type=jnp.float32)
        + jnp.einsum("hpk,khe->phe", prev_ds, keys_prev, preferred_element_type=jnp.float32)
    ).astype(jnp.bfloat16)
    key_own_g = jnp.einsum("hpk,phe->khe", own_ds, queries, preferred_element_type=jnp.float32)
    value_own_g = jnp.einsum(
        "hpk,phe->khe", own_p.astype(jnp.bfloat16), grad_attn, preferred_element_type=jnp.float32
    )
    key_back_g = jnp.einsum(
        "hpk,phe->khe", prev_ds, queries, preferred_element_type=jnp.float32
    ).astype(jnp.bfloat16)
    value_back_g = jnp.einsum(
        "hpk,phe->khe", prev_p.astype(jnp.bfloat16), grad_attn, preferred_element_type=jnp.float32
    ).astype(jnp.bfloat16)
    key_next, value_next = from_behind((key_back_g, value_back_g), "tm", -1)
    grad_key = (key_own_g + key_next.astype(jnp.float32)).astype(jnp.bfloat16)
    grad_value = (value_own_g + value_next.astype(jnp.float32)).astype(jnp.bfloat16)
    grad_qkv = jnp.concatenate(
        [
            grad_query.reshape(frame_len, local_width),
            grad_key.reshape(frame_len, local_width),
            grad_value.reshape(frame_len, local_width),
        ],
        axis=1,
    )
    grad_hidden = lax.psum_scatter(
        lax.dot_general(
            grad_qkv, flat_w, (((1,), (1,)), ((), ())), preferred_element_type=jnp.float32
        ).astype(jnp.bfloat16),
        "head",
        scatter_dimension=0,
        tiled=True,
    ).astype(jnp.float32)
    grad_normed = grad_hidden * norm_gain
    inner = jnp.mean(grad_normed * normed, axis=-1, keepdims=True)
    result = cotangent.astype(jnp.float32) + inv_rms * (grad_normed - normed * inner)
    return result.astype(jnp.bfloat16)


def solution(mesh):
    return jax.shard_map(
        shards,
        mesh=mesh,
        in_specs=(
            P(("tm", "head"), None),
            P(("tm", "head"), None),
            P(),
            P(None, None, "head"),
            P("head", None),
        ),
        out_specs=P(("tm", "head"), None),
        check_vma=False,
    )
```

profile of v0, /device:TPU:8, one launch (start us, length us, event | category | flops | bytes accessed | tf_op | source)
XLA Modules:
  0.0 347.7 jit_solution(16157256869247840403)
XLA Ops:
  6.5 1.3 fusion.33
  7.9 1.9 fusion.27
  10.6 10.3 %copy.24 = bf16[3072,3,384]{0,2,1:T(8,128)(2,1)} copy(bf16[3072,3,384]{2,0,1:T(8,128)(2,1)} %param.8) | data formatting | bytes 14155776 | tf_op args[3]
  20.9 83.8 %all-gather.3.cloned.1.call-done = bf16[512,3072]{1,0:T(8,128)(2,1)} async-done(((bf16[64,3072]{1,0:T(8,128)(2,1)}), bf16[512,3072]{1,0:T(8,128)(2,1)}) %all-gather.3.cloned.1.call-update) | async-done | bytes 3145744 | tf_op jit(solution)/shard_map/all_gather | solution.py:33
  104.7 8.2 %convolution_convert_fusion.1 = bf16[512,1152]{1,0:T(8,128)(2,1)S(1)} fusion(bf16[512,3072]{1,0:T(8,128)(2,1)} %all-gather.3.cloned.1.call-done, bf16[3072,1152]{0,1:T(8,128)(2,1)} %bitcast.47), kind=kOutput, calls=%fused_computation.7 | convolution fusion | flops 3624468480 | bytes 11403264 | tf_op jit(solution)/shard_map/dot_general | solution.py:32
  114.0 0.9 copy.34
  114.9 1.2 copy.25
  117.0 1.9 collective-permute-start
  118.9 2.6 collective-permute-start.1
  121.6 73.9 %all-gather.5.cloned.1.call-done = bf16[512,3072]{1,0:T(8,128)(2,1)} async-done(((bf16[64,3072]{1,0:T(8,128)(2,1)}), bf16[512,3072]{1,0:T(8,128)(2,1)}) %all-gather.5.cloned.1.call-update) | async-done | bytes 3145744 | tf_op jit(solution)/shard_map/all_gather | solution.py:46
  195.5 3.3 convolution_convert_fusion.3
  198.8 2.3 fusion.40
  202.0 1.6 multiply_reduce_fusion.2
  203.6 1.1 fusion.3
  205.7 2.1 collective-permute-start.3
  207.9 2.7 multiply_reduce_fusion
  210.6 2.0 multiply_convert_fusion
  213.6 1.9 collective-permute-start.2
  215.5 1.6 fusion.14
  218.0 2.8 collective-permute-done.2
  221.5 5.8 %convolution_convert_fusion = bf16[512,3072]{1,0:T(8,128)(2,1)} fusion(bf16[3072,1152]{0,1:T(8,128)(2,1)S(1)} %bitcast.50, bf16[512,384]{0,1:T(8,128)(2,1)S(1)} %bitcast.62, bf16[512,384]{0,1:T(8,128)(2,1)S(1)} %bitcast.57, bf16[512,384]{0,1:T(8,128)(2,1)S(1)} %bitcast.56), kind=kOutput, calls=%fused_computation | convolution fusion | flops 3628990464 | bytes 11403264 | tf_op jit(solution)/shard_map/dot_general | solution.py:95
  227.3 110.5 %reduce-scatter.2.cloned.1.call-done = bf16[64,3072]{1,0:T(8,128)(2,1)} async-done(((bf16[512,3072]{1,0:T(8,128)(2,1)}), bf16[64,3072]{1,0:T(8,128)(2,1)}) %reduce-scatter.2.cloned.1.call-update) | async-done | bytes 393232 | tf_op jit(solution)/shard_map/reduce_scatter | solution.py:94
  337.8 1.3 fusion.28
  339.1 2.0 fusion.32
  (43 shorter events, 7.1 us)
Async XLA Ops:
  6.5 189.0 %copy-start = (bf16[384,3072]{1,0:T(8,128)(2,1)S(1)}, bf16[384,3072]{1,0:T(8,128)(2,1)}, u32[]{:S(2)}) copy-start(bf16[384,3072]{1,0:T(8,128)(2,1)} %param.9) | copy-start | bytes 7077892
  6.5 98.1 %all-gather.3.cloned.1.call-start = ((), (), s32[]{:S(2)}) async-start(), calls=%async_computation.1 | async-start | bytes 3538944 | tf_op jit(solution)/shard_map/all_gather | solution.py:33
  9.8 185.7 %all-gather.5.cloned.1.call-start = ((), (), s32[]{:S(2)}) async-start(), calls=%async_computation.2 | async-start | bytes 3538944 | tf_op jit(solution)/shard_map/all_gather | solution.py:46
  10.6 327.2 %reduce-scatter.2.cloned.1.call-start = ((), (), s32[]{:S(2)}) async-start(), calls=%async_computation.3 | async-start | bytes 3538944 | tf_op jit(solution)/shard_map/reduce_scatter | solution.py:94
  117.0 85.0 %collective-permute-start = (bf16[512,3,128]{2,0,1:T(8,128)(2,1)}, bf16[512,3,128]{2,0,1:T(8,128)(2,1)}, u32[]{:S(2)}, u32[]{:S(2)}) collective-permute-start(bf16[512,3,128]{2,0,1:T(8,128)(2,1)} %copy.29), channel_id=1, source_target_pairs={{0,8},{8,16},{16,24},{24,32},{32,40},{40,48},{48,56},{56,64},{64,7... | collective-permute-start | bytes 1179656 | tf_op jit(solution)/shard_map/ppermute | solution.py:13
  118.9 88.9 %collective-permute-start.1 = (bf16[512,3,128]{2,0,1:T(8,128)(2,1)}, bf16[512,3,128]{2,0,1:T(8,128)(2,1)}, u32[]{:S(2)}, u32[]{:S(2)}) collective-permute-start(bf16[512,3,128]{2,0,1:T(8,128)(2,1)} %copy.34), channel_id=1, source_target_pairs={{0,8},{8,16},{16,24},{24,32},{32,40},{40,48},{48,56},{56,64},{64,7... | collective-permute-start | bytes 1179656 | tf_op jit(solution)/shard_map/ppermute | solution.py:13
  198.8 2.4 copy-start.4
  203.6 1.2 copy-start.5
  204.8 3.1 copy-start.1
  205.7 11.4 %collective-permute-start.3 = (bf16[512,3,128]{0,2,1:T(8,128)(2,1)S(1)}, bf16[512,3,128]{0,2,1:T(8,128)(2,1)S(1)}, u32[]{:S(2)}, u32[]{:S(2)}) collective-permute-start(bf16[512,3,128]{0,2,1:T(8,128)(2,1)S(1)} %fusion.16), channel_id=1, source_target_pairs={{8,0},{16,8},{24,16},{32,24},{40,32},{48,40},{56,48},{64,56},{72,6... | collective-permute-start | bytes 1179656 | tf_op jit(solution)/shard_map/ppermute | solution.py:13
  213.6 7.2 %collective-permute-start.2 = (bf16[512,3,128]{0,2,1:T(8,128)(2,1)S(1)}, bf16[512,3,128]{0,2,1:T(8,128)(2,1)S(1)}, u32[]{:S(2)}, u32[]{:S(2)}) collective-permute-start(bf16[512,3,128]{0,2,1:T(8,128)(2,1)S(1)} %fusion.15), channel_id=1, source_target_pairs={{8,0},{16,8},{24,16},{32,24},{40,32},{48,40},{56,48},{64,56},{72,6... | collective-permute-start | bytes 1179656 | tf_op jit(solution)/shard_map/ppermute | solution.py:13
  215.5 5.9 %slice-start = ((s8[7077888]{0:T(1024)(128)(4,1)}), s8[2883584]{0:T(1024)(128)(4,1)S(1)}, s32[]{:S(2)}) async-start(s8[7077888]{0:T(1024)(128)(4,1)} %bitcast.48), calls=%async_computation.4 | async-start | bytes 5767168
  217.1 4.3 %slice-start.1 = ((s8[7077888]{0:T(1024)(128)(4,1)}), s8[4194304]{0:T(1024)(128)(4,1)S(1)}, s32[]{:S(2)}) async-start(s8[7077888]{0:T(1024)(128)(4,1)} %bitcast.48), calls=%async_computation.5 | async-start | bytes 8388608
  227.3 110.5 %copy-start.2 = (bf16[64,3072]{1,0:T(8,128)(2,1)S(1)}, bf16[64,3072]{1,0:T(8,128)(2,1)}, u32[]{:S(2)}) copy-start(bf16[64,3072]{1,0:T(8,128)(2,1)} %param.5) | copy-start | bytes 1179652
  227.3 110.5 %copy-start.6 = (f32[3072]{0:T(1024)S(1)}, f32[3072]{0:T(1024)}, u32[]{:S(2)}) copy-start(f32[3072]{0:T(1024)} %param.7) | copy-start | bytes 36868
  227.3 111.8 %copy-start.3 = (bf16[64,3072]{1,0:T(8,128)(2,1)S(1)}, bf16[64,3072]{1,0:T(8,128)(2,1)}, u32[]{:S(2)}) copy-start(bf16[64,3072]{1,0:T(8,128)(2,1)} %param.6) | copy-start | bytes 1179652
Sparse Core Ops, SparseCore 0:
  10.0 94.6 all-gather.2
  107.3 88.1 all-gather.4
  227.4 110.3 reduce-scatter.1
where the time goes:
time: 348 us
  waiting for transfers between devices  272 us (78%)
  matrix products  29.5 us (8%)
  local copies, waits for them, and re-layouts  14.6 us (4%)
  between operations  13.4 us (4%)
  other arithmetic  9.71 us (3%)
  starting transfers between devices  8.65 us (2%)
    reduce_scatter x1, waiting for transfers between devices, shards(): lax.psum_scatter(lax.dot_general(grad_qkv, flat_w, (((1,), (1,)), ((), ()...  110 us
    all_gather x1, waiting for transfers between devices, shards(): lax.all_gather(hidden, 'head', axis=0, tiled=True)  83.8 us
    all_gather x1, waiting for transfers between devices, shards(): lax.all_gather(cotangent, 'head', axis=0, tiled=True)  73.9 us
    unnamed x19, local copies, waits for them, and re-layouts  10.3 us
    ppermute x4, starting transfers between devices, from_behind(): return lax.ppermute(block, axis, route)  8.57 us
    dot_general x1, matrix products, shards(): jnp.dot(lax.all_gather(hidden, 'head', axis=0, tiled=True), flat_w, prefe...  8.22 us
  transfers between devices with their start and end apart: 7, of which 4 were waited for; matrix products, arithmetic and copies ran while one was open for 12% of the time, Pallas kernels for 0%

commit v1 on v0

--- a/solution.py
+++ b/solution.py
@@ -29,10 +29,14 @@
     normed = latent_f * inv_rms
     hidden = (normed * norm_gain).astype(jnp.bfloat16)
     flat_w = w_qkv.reshape(feature_count, 3 * local_width)
+
+    def _direct_classes(z, lane_axis, in_dim):
+        response = jnp.stack(lax.axis_size(lane_axis) * [z], axis=0)
+        local_next = lax.all_to_all(response, lane_axis, 0, 0)
+        return jnp.concatenate(local_next, axis=in_dim)
+
     projected = jnp.dot(
-        lax.all_gather(hidden, "head", axis=0, tiled=True),
-        flat_w,
-        preferred_element_type=jnp.float32,
+        _direct_classes(hidden, "head", 0), flat_w, preferred_element_type=jnp.float32
     ).astype(jnp.bfloat16)
     frame_len = projected.shape[0]
     shape3 = (frame_len, heads_here, HEAD_DIM)

time: 348 us -> 317 us (0.911)
  waiting for transfers between devices: 272 us -> 222 us
  starting transfers between devices: 8.65 us -> 24.1 us
    all_gather x1 -> x0, waiting for transfers between devices: 83.8 us -> none  [shards(): lax.all_gather(hidden, 'head', axis=0, tiled=True)]
    all_to_all x0 -> x1, waiting for transfers between devices: none -> 70.6 us  [_direct_classes(): local_next = lax.all_to_all(response, lane_axis, 0, 0)]
    all_gather x1, waiting for transfers between devices: 73.9 us -> 36 us  [shards(): lax.all_gather(cotangent, 'head', axis=0, tiled=True)]
    all_to_all x0 -> x1, starting transfers between devices: none -> 10.9 us  [_direct_classes(): local_next = lax.all_to_all(response, lane_axis, 0, 0)]
    ppermute x4, starting transfers between devices: 8.57 us -> 13.1 us  [from_behind(): return lax.ppermute(block, axis, route)]
  transfers between devices with their start and end apart: 7 -> 7, of which waited for: 4 -> 4; matrix products, arithmetic and copies ran while one was open for 12% -> 13% of each run, Pallas kernels for 0% -> 0%
where the time goes in v1:
time: 317 us; the launch traced here: 316 us
  waiting for transfers between devices  222 us (70%)
  matrix products  30 us (9%)
  starting transfers between devices  24.1 us (8%)
  local copies, waits for them, and re-layouts  16.6 us (5%)
  between operations  13.7 us (4%)
  other arithmetic  8.96 us (3%)
    reduce_scatter x1, waiting for transfers between devices, shards(): lax.psum_scatter(lax.dot_general(grad_qkv, flat_w, (((1,), (1,)), ((), ()...  112 us
    all_to_all x1, waiting for transfers between devices, _direct_classes(): local_next = lax.all_to_all(response, lane_axis, 0, 0)  70.6 us
    all_gather x1, waiting for transfers between devices, shards(): lax.all_gather(cotangent, 'head', axis=0, tiled=True)  36 us
    ppermute x4, starting transfers between devices, from_behind(): return lax.ppermute(block, axis, route)  13.1 us
    all_to_all x1, starting transfers between devices, _direct_classes(): local_next = lax.all_to_all(response, lane_axis, 0, 0)  10.9 us
    unnamed x19, local copies, waits for them, and re-layouts  10.3 us
    dot_general x1, matrix products, shards(): jnp.dot(_direct_classes(hidden, 'head', 0), flat_w, preferred_element_typ...  8.62 us
  transfers between devices with their start and end apart: 7, of which 4 were waited for; matrix products, arithmetic and copies ran while one was open for 13% of the time, Pallas kernels for 0%

profile of v1, /device:TPU:8, one launch (start us, length us, event | category | flops | bytes accessed | tf_op | source)
XLA Modules:
  0.0 315.9 jit_solution(13763728435365207676)
XLA Ops:
  6.5 1.3 fusion.33
  7.9 1.2 fusion.27
  9.0 2.0 stack.2
  11.1 10.9 %all-to-all-start = ((bf16[8,64,3072]{2,1,0:T(8,128)(2,1)}), bf16[8,64,3072]{2,1,0:T(8,128)(2,1)}, u32[]{:S(2)}, u32[]{:S(2)}) async-start(bf16[8,64,3072]{2,1,0:T(8,128)(2,1)} %stack.2), calls=%async_computation | async-start | bytes 6291456 | tf_op jit(solution)/shard_map/all_to_all | solution.py:35
  22.8 10.3 %copy.24 = bf16[3072,3,384]{0,2,1:T(8,128)(2,1)} copy(bf16[3072,3,384]{2,0,1:T(8,128)(2,1)} %param.8) | data formatting | bytes 14155776 | tf_op args[3]
  33.0 70.6 %all-to-all-done = bf16[8,64,3072]{2,1,0:T(8,128)(2,1)} async-done(((bf16[8,64,3072]{2,1,0:T(8,128)(2,1)}), bf16[8,64,3072]{2,1,0:T(8,128)(2,1)}, u32[]{:S(2)}, u32[]{:S(2)}) %all-to-all-start) | async-done | bytes 3145760 | tf_op jit(solution)/shard_map/all_to_all | solution.py:35
  103.7 8.6 %convolution_convert_fusion.1 = bf16[512,1152]{1,0:T(8,128)(2,1)S(1)} fusion(bf16[512,3072]{1,0:T(8,128)(2,1)} %bitcast, bf16[3072,1152]{0,1:T(8,128)(2,1)} %bitcast.48), kind=kOutput, calls=%fused_computation.7 | convolution fusion | flops 3624468480 | bytes 11403264 | tf_op jit(solution)/shard_map/dot_general | solution.py:38
  114.3 1.2 copy.25
  116.4 1.9 collective-permute-start
  118.3 3.1 collective-permute-start.1
  121.4 36.0 %all-gather.2.cloned.1.call-done = bf16[512,3072]{1,0:T(8,128)(2,1)} async-done(((bf16[64,3072]{1,0:T(8,128)(2,1)}), bf16[512,3072]{1,0:T(8,128)(2,1)}) %all-gather.2.cloned.1.call-update) | async-done | bytes 3145744 | tf_op jit(solution)/shard_map/all_gather | solution.py:50
  157.4 3.3 %convolution_convert_fusion.3 = bf16[512,384]{0,1:T(8,128)(2,1)S(1)} fusion(bf16[512,3072]{1,0:T(8,128)(2,1)} %all-gather.2.cloned.1.call-done, bf16[384,3072]{1,0:T(8,128)(2,1)S(1)} %copy-done), kind=kOutput, calls=%fused_computation.23 | convolution fusion | flops 1208156160 | bytes 5898240 | tf_op jit(solution)/shard_map/dot_general | solution.py:49
  160.7 2.3 fusion.40
  163.9 1.6 multiply_reduce_fusion.2
  167.6 5.3 %collective-permute-start.3 = (bf16[512,3,128]{0,2,1:T(8,128)(2,1)S(1)}, bf16[512,3,128]{0,2,1:T(8,128)(2,1)S(1)}, u32[]{:S(2)}, u32[]{:S(2)}) collective-permute-start(bf16[512,3,128]{0,2,1:T(8,128)(2,1)S(1)} %fusion.16), channel_id=1, source_target_pairs={{8,0},{16,8},{24,16},{32,24},{40,32},{48,40},{56,48},{64,56},{72,6... | collective-permute-start | bytes 1179656 | tf_op jit(solution)/shard_map/ppermute | solution.py:13
  173.0 2.7 multiply_reduce_fusion
  175.7 2.0 multiply_convert_fusion
  178.7 2.8 collective-permute-start.2
  181.6 1.6 fusion.14
  184.0 2.8 collective-permute-done.2
  187.5 5.8 %convolution_convert_fusion = bf16[512,3072]{1,0:T(8,128)(2,1)} fusion(bf16[3072,1152]{0,1:T(8,128)(2,1)S(1)} %bitcast.51, bf16[512,384]{0,1:T(8,128)(2,1)S(1)} %bitcast.63, bf16[512,384]{0,1:T(8,128)(2,1)S(1)} %bitcast.58, bf16[512,384]{0,1:T(8,128)(2,1)S(1)} %bitcast.57), kind=kOutput, calls=%fused_computation | convolution fusion | flops 3628990464 | bytes 11403264 | tf_op jit(solution)/shard_map/dot_general | solution.py:99
  193.4 112.3 %reduce-scatter.2.cloned.1.call-done = bf16[64,3072]{1,0:T(8,128)(2,1)} async-done(((bf16[512,3072]{1,0:T(8,128)(2,1)}), bf16[64,3072]{1,0:T(8,128)(2,1)}) %reduce-scatter.2.cloned.1.call-update) | async-done | bytes 393232 | tf_op jit(solution)/shard_map/reduce_scatter | solution.py:98
  305.7 1.3 fusion.28
  307.0 2.0 fusion.32
  (43 shorter events, 9.2 us)
Async XLA Ops:
  6.5 150.9 %copy-start = (bf16[384,3072]{1,0:T(8,128)(2,1)S(1)}, bf16[384,3072]{1,0:T(8,128)(2,1)}, u32[]{:S(2)}) copy-start(bf16[384,3072]{1,0:T(8,128)(2,1)} %param.9) | copy-start | bytes 7077892
  11.1 92.6 %all-to-all-start = ((bf16[8,64,3072]{2,1,0:T(8,128)(2,1)}), bf16[8,64,3072]{2,1,0:T(8,128)(2,1)}, u32[]{:S(2)}, u32[]{:S(2)}) async-start(bf16[8,64,3072]{2,1,0:T(8,128)(2,1)} %stack.2), calls=%async_computation | async-start | bytes 6291456 | tf_op jit(solution)/shard_map/all_to_all | solution.py:35
  22.0 135.4 %all-gather.2.cloned.1.call-start = ((), (), s32[]{:S(2)}) async-start(), calls=%async_computation.2 | async-start | bytes 3538944 | tf_op jit(solution)/shard_map/all_gather | solution.py:50
  22.7 283.0 %reduce-scatter.2.cloned.1.call-start = ((), (), s32[]{:S(2)}) async-start(), calls=%async_computation.3 | async-start | bytes 3538944 | tf_op jit(solution)/shard_map/reduce_scatter | solution.py:98
  116.4 47.5 %collective-permute-start = (bf16[512,3,128]{2,0,1:T(8,128)(2,1)}, bf16[512,3,128]{2,0,1:T(8,128)(2,1)}, u32[]{:S(2)}, u32[]{:S(2)}) collective-permute-start(bf16[512,3,128]{2,0,1:T(8,128)(2,1)} %copy.29), channel_id=1, source_target_pairs={{0,8},{8,16},{16,24},{24,32},{32,40},{40,48},{48,56},{56,64},{64,7... | collective-permute-start | bytes 1179656 | tf_op jit(solution)/shard_map/ppermute | solution.py:13
  118.3 54.6 %collective-permute-start.1 = (bf16[512,3,128]{2,0,1:T(8,128)(2,1)}, bf16[512,3,128]{2,0,1:T(8,128)(2,1)}, u32[]{:S(2)}, u32[]{:S(2)}) collective-permute-start(bf16[512,3,128]{2,0,1:T(8,128)(2,1)} %copy.34), channel_id=1, source_target_pairs={{0,8},{8,16},{16,24},{24,32},{32,40},{40,48},{48,56},{56,64},{64,7... | collective-permute-start | bytes 1179656 | tf_op jit(solution)/shard_map/ppermute | solution.py:13
  160.7 2.4 copy-start.4
  165.5 1.2 copy-start.5
  166.7 6.3 %copy-start.1 = (f32[3,512,512]{1,2,0:T(8,128)S(1)}, f32[3,512,512]{1,2,0:T(8,128)}, u32[]{:S(2)}) copy-start(f32[3,512,512]{1,2,0:T(8,128)} %fusion.40) | copy-start | bytes 9437188
  167.6 15.5 %collective-permute-start.3 = (bf16[512,3,128]{0,2,1:T(8,128)(2,1)S(1)}, bf16[512,3,128]{0,2,1:T(8,128)(2,1)S(1)}, u32[]{:S(2)}, u32[]{:S(2)}) collective-permute-start(bf16[512,3,128]{0,2,1:T(8,128)(2,1)S(1)} %fusion.16), channel_id=1, source_target_pairs={{8,0},{16,8},{24,16},{32,24},{40,32},{48,40},{56,48},{64,56},{72,6... | collective-permute-start | bytes 1179656 | tf_op jit(solution)/shard_map/ppermute | solution.py:13
  178.7 8.1 %collective-permute-start.2 = (bf16[512,3,128]{0,2,1:T(8,128)(2,1)S(1)}, bf16[512,3,128]{0,2,1:T(8,128)(2,1)S(1)}, u32[]{:S(2)}, u32[]{:S(2)}) collective-permute-start(bf16[512,3,128]{0,2,1:T(8,128)(2,1)S(1)} %fusion.15), channel_id=1, source_target_pairs={{8,0},{16,8},{24,16},{32,24},{40,32},{48,40},{56,48},{64,56},{72,6... | collective-permute-start | bytes 1179656 | tf_op jit(solution)/shard_map/ppermute | solution.py:13
  181.5 5.9 %slice-start = ((s8[7077888]{0:T(1024)(128)(4,1)}), s8[2883584]{0:T(1024)(128)(4,1)S(1)}, s32[]{:S(2)}) async-start(s8[7077888]{0:T(1024)(128)(4,1)} %bitcast.49), calls=%async_computation.4 | async-start | bytes 5767168
  183.1 4.4 %slice-start.1 = ((s8[7077888]{0:T(1024)(128)(4,1)}), s8[4194304]{0:T(1024)(128)(4,1)S(1)}, s32[]{:S(2)}) async-start(s8[7077888]{0:T(1024)(128)(4,1)} %bitcast.49), calls=%async_computation.5 | async-start | bytes 8388608
  193.3 112.4 %copy-start.2 = (bf16[64,3072]{1,0:T(8,128)(2,1)S(1)}, bf16[64,3072]{1,0:T(8,128)(2,1)}, u32[]{:S(2)}) copy-start(bf16[64,3072]{1,0:T(8,128)(2,1)} %param.5) | copy-start | bytes 1179652
  193.3 112.4 %copy-start.6 = (f32[3072]{0:T(1024)S(1)}, f32[3072]{0:T(1024)}, u32[]{:S(2)}) copy-start(f32[3072]{0:T(1024)} %param.7) | copy-start | bytes 36868
  193.3 113.7 %copy-start.3 = (bf16[64,3072]{1,0:T(8,128)(2,1)S(1)}, bf16[64,3072]{1,0:T(8,128)(2,1)}, u32[]{:S(2)}) copy-start(bf16[64,3072]{1,0:T(8,128)(2,1)} %param.6) | copy-start | bytes 1179652
Sparse Core Ops, SparseCore 0:
  25.4 131.9 all-gather.1
  193.5 112.1 reduce-scatter.1
